TPU v7x, 32 devices: a whole 2x2x4 slice. The times are simulated.
32 devices in a mesh: grp: 2 (over x), ad: 16 (over z, y, core).
Axes of the slice: x: 2, y: 2, z: 4, core: 2. Of those that a mesh axis runs over, the one named last changes fastest.
Arguments:
- queries: bfloat16 [1024, 4096], P(('grp', 'ad')), parts along dimension 0, may hold values from -100 to 100
- cached_key_vectors: bfloat16 [1024, 64, 512], P(('grp', 'ad')), parts along dimension 0, may hold values from -4 to 4
- stored_values: bfloat16 [1024, 64, 512], P(('grp', 'ad')), parts along dimension 0, may hold values from -12 to 12
- lengths: int32 [1024], P(('grp', 'ad')), parts along dimension 0, may hold values from 2 to 64, as said below
- request_adapters: int32 [1024], P(('grp', 'ad')), parts along dimension 0, may hold values from 0 to 63, as said below
- output_weight_rows: bfloat16 [4096, 8192], P(None, 'ad'), may hold values from -0.09375 to 0.09375
- adapter_down_maps: bfloat16 [4096, 4096], P(None, 'ad'), may hold values from -0.09375 to 0.09375
- adapter_up_maps: bfloat16 [4096, 8192], P('ad'), may hold values from -0.75 to 0.75
Outputs:
- layer_out: bfloat16 [1024, 8192], P(('grp', 'ad')), parts along dimension 0
There are 2 independent parts, one for each index of `grp`. A program takes and returns all parts, laid end to end along the dimension named above; an argument that names none is the same for every part. Nothing has to cross between parts.
Inputs may be any that keep to these rules, and one draw needn't show every extreme that they name: `lengths`: each device's block of 32 requests holds one of length 64. `request_adapters`: adapter a is held by device a // 4 of ad. Among the 32 requests of one device, each holding device that is named is named by exactly 2 of them; one holding device is named so by every device.
All inputs are finite; a program needn't handle non-finite values.
Results may differ from a plain program's by a relative error of at most 0.014.
Values may be sent and summed in bfloat16 or wider, within the bound.
A program may use at most 128 MiB of HBM per device.

v0:
```python
import jax
import jax.numpy as jnp
from jax import lax
from jax.sharding import PartitionSpec as P

LOCAL_HEADS = 32
KV_HEADS = 4
HEAD_SIZE = 128
ADAPTER_RANK = 64
CAP = 2


def attend(queries, cached_key_vectors, stored_values, lengths):
    request_count, positions, kv_width = cached_key_vectors.shape
    group_size = LOCAL_HEADS // KV_HEADS
    query_heads = queries.reshape(request_count, KV_HEADS, group_size, HEAD_SIZE)
    key_heads = cached_key_vectors.reshape(request_count, positions, KV_HEADS, HEAD_SIZE)
    value_heads = stored_values.reshape(request_count, positions, KV_HEADS, HEAD_SIZE)
    scores = jnp.einsum(
        "rkgh,rckh->rkgc", query_heads, key_heads, preferred_element_type=jnp.float32
    ) * HEAD_SIZE ** (-0.5)
    live_mask = (jnp.arange(positions, dtype=jnp.int32)[None, :] < lengths[:, None])[
        :, None, None, :
    ]
    scores = jnp.where(live_mask, scores, jnp.float32(-1e30))
    row_max = jnp.max(scores, axis=-1, keepdims=True)
    exp_scores = jnp.where(live_mask, jnp.exp(scores - row_max), jnp.float32(0.0))
    probs = (exp_scores / jnp.sum(exp_scores, axis=-1, keepdims=True)).astype(jnp.bfloat16)
    attended = jnp.einsum("rkgc,rckh->rkgh", probs, value_heads, preferred_element_type=jnp.float32)
    return attended.reshape(request_count, LOCAL_HEADS * HEAD_SIZE).astype(jnp.bfloat16)


def slot_ranks(owner_of):
    row_count = owner_of.shape[-1]
    same_owner = owner_of[..., :, None] == owner_of[..., None, :]
    earlier = jnp.arange(row_count)[None, :] < jnp.arange(row_count)[:, None]
    return jnp.sum(same_owner & earlier, axis=-1)


def adapter_positions(
    position_rows, position_index, adapter_down_maps, adapter_up_maps, leading_adapter
):
    source_devices, position_count, row_width = position_rows.shape
    local_id = (position_index - leading_adapter).reshape(source_devices * position_count)
    shrunk_all = jnp.dot(
        position_rows.reshape(source_devices * position_count, row_width),
        adapter_down_maps,
        preferred_element_type=jnp.float32,
    )
    block_lookup = jnp.arange(adapter_down_maps.shape[1], dtype=jnp.int32) // ADAPTER_RANK
    own_block = block_lookup[None, :] == local_id[:, None]
    reduced_rows = jnp.where(own_block, shrunk_all, jnp.float32(0.0)).astype(jnp.bfloat16)
    delta_outputs = jnp.dot(
        reduced_rows, adapter_up_maps, preferred_element_type=jnp.float32
    ).astype(jnp.bfloat16)
    return delta_outputs.reshape(source_devices, position_count, adapter_up_maps.shape[1])


def send_back(delta_outputs):
    return lax.all_to_all(delta_outputs, "ad", split_axis=0, concat_axis=0, tiled=True)


def local(
    queries,
    cached_key_vectors,
    stored_values,
    lengths,
    request_adapters,
    output_weight_rows,
    adapter_down_maps,
    adapter_up_maps,
):
    attended = attend(queries, cached_key_vectors, stored_values, lengths)
    my_index = lax.axis_index("ad")
    peer_count = lax.axis_size("ad")
    device_share = adapter_down_maps.shape[1] // ADAPTER_RANK
    leading_adapter = my_index * device_share
    owner_of = request_adapters // device_share
    slot_rank = slot_ranks(owner_of)
    slot_pick = (
        owner_of[None, None, :] == jnp.arange(peer_count, dtype=jnp.int32)[:, None, None]
    ) & (slot_rank[None, None, :] == jnp.arange(CAP, dtype=jnp.int32)[None, :, None])
    pick_matrix = slot_pick.astype(jnp.bfloat16)
    send_rows = jnp.einsum(
        "ocr,rd->ocd", pick_matrix, attended, preferred_element_type=jnp.float32
    ).astype(jnp.bfloat16)
    send_ids = jnp.sum(jnp.where(slot_pick, request_adapters[None, None, :] + 1, 0), axis=-1) - 1
    returned = send_back(
        adapter_positions(
            lax.all_to_all(send_rows, "ad", split_axis=0, concat_axis=0, tiled=True),
            lax.all_to_all(send_ids, "ad", split_axis=0, concat_axis=0, tiled=True),
            adapter_down_maps,
            adapter_up_maps,
            leading_adapter,
        )
    )
    base_cols = jnp.dot(
        lax.all_gather(attended, "ad", axis=0, tiled=True),
        output_weight_rows,
        preferred_element_type=jnp.float32,
    )
    delta_rows = jnp.einsum(
        "ocr,ocd->rd", pick_matrix, returned, preferred_element_type=jnp.float32
    )
    base_rows = lax.all_to_all(base_cols, "ad", split_axis=0, concat_axis=1, tiled=True)
    return (base_rows + delta_rows).astype(jnp.bfloat16)


def solution(mesh):
    return jax.shard_map(
        local,
        mesh=mesh,
        in_specs=(
            P(("grp", "ad"), None),
            P(("grp", "ad"), None, None),
            P(("grp", "ad"), None, None),
            P(("grp", "ad")),
            P(("grp", "ad")),
            P(None, "ad"),
            P(None, "ad"),
            P("ad", None),
        ),
        out_specs=P(("grp", "ad"), None),
        check_vma=False,
    )
```

profile of v0, /device:TPU:9, one launch (start us, length us, event | category | flops | bytes accessed | tf_op | source)
XLA Modules:
  0.0 134.7 jit_solution(17900416777147413588)
XLA Ops:
  6.5 0.0 copy-start
  6.5 0.0 all-gather.2.cloned.1.call-start
  6.5 0.9 iota_compare_fusion.1
  7.4 1.0 copy.35
  8.4 3.0 %fusion.37 = (f32[32,4,8]{2,1,0:T(4,128)S(1)}, f32[32,4,8,64]{3,2,1,0:T(8,128)S(1)}) fusion(pred[32,64]{1,0:T(8,128)(4,1)S(1)} %iota_compare_fusion.1, bf16[32,4,8,128]{3,2,1,0:T(8,128)(2,1)S(1)} %bitcast.58, bf16[32,64,512]{2,1,0:T(8,128)(2,1)} %param.9), kind=kOutput, calls=%fused_computation.54 | convolution fusion | flops 17104960 | bytes 2627584 | tf_op jit(solution)/shard_map/sub | solution.py:27
  11.4 0.0 copy-start.1
  11.4 2.3 %fusion.18 = bf16[32,4,8,128]{3,2,1,0:T(8,128)(2,1)S(1)} fusion(f32[32,4,8,64]{3,2,1,0:T(8,128)S(1)} %get-tuple-element.8, f32[32,4,8]{2,1,0:T(4,128)S(1)} %get-tuple-element.7, bf16[32,64,512]{2,1,0:T(8,128)(2,1)} %param.10), kind=kOutput, calls=%fused_computation.17 | convolution fusion | flops 17039360 | bytes 2625536 | tf_op jit(solution)/shard_map/rkgc,rckh->rkgh/dot_general | solution.py:29
  13.7 0.8 copy.56
  14.5 0.0 all-gather.2.cloned.1.call-update
  14.6 0.0 copy-done.1
  14.6 0.2 convert_reduce_fusion
  14.8 0.1 fusion.27
  14.9 0.7 copy.29
  15.6 6.6 %all-to-all-start.1 = ((s32[16,1,2]{2,1,0:T(1,128)}), s32[16,1,2]{2,1,0:T(1,128)S(1)}, u32[]{:S(2)}, u32[]{:S(2)}) async-start(s32[16,1,2]{2,1,0:T(1,128)} %copy.29), calls=%async_computation.1 | async-start | bytes 16384 | tf_op jit(solution)/shard_map/all_to_all | solution.py:91
  22.2 0.1 reshape.125
  22.3 0.2 convolution_convert_fusion.1
  22.5 1.0 copy.30
  23.5 3.4 %all-to-all-done.1 = s32[16,1,2]{2,1,0:T(1,128)S(1)} async-done(((s32[16,1,2]{2,1,0:T(1,128)}), s32[16,1,2]{2,1,0:T(1,128)S(1)}, u32[]{:S(2)}, u32[]{:S(2)}) %all-to-all-start.1) | async-done | bytes 160 | tf_op jit(solution)/shard_map/all_to_all | solution.py:91
  26.9 5.2 %all-to-all-start.2 = ((bf16[16,2,4096]{2,1,0:T(2,128)(2,1)}), bf16[16,2,4096]{2,1,0:T(2,128)(2,1)S(1)}, u32[]{:S(2)}, u32[]{:S(2)}) async-start(bf16[16,2,4096]{2,1,0:T(2,128)(2,1)} %copy.30), calls=%async_computation.2 | async-start | bytes 524288 | tf_op jit(solution)/shard_map/all_to_all | solution.py:90
  32.1 38.4 %all-gather.2.cloned.1.call-done = bf16[512,4096]{1,0:T(8,128)(2,1)} async-done(((bf16[32,4096]{1,0:T(8,128)(2,1)}), bf16[512,4096]{1,0:T(8,128)(2,1)}) %all-gather.2.cloned.1.call-update) | async-done | bytes 4194320 | tf_op jit(solution)/shard_map/all_gather | solution.py:98
  70.5 6.8 %fusion.40 = f32[512,512]{1,0:T(8,128)} fusion(bf16[512,4096]{1,0:T(8,128)(2,1)} %all-gather.2.cloned.1.call-done, bf16[4096,512]{1,0:T(8,128)(2,1)} %param.13), kind=kOutput, calls=%fused_computation.55 | convolution fusion | flops 2147483648 | bytes 9437184 | tf_op jit(solution)/shard_map/dot_general | solution.py:97
  77.3 0.0 all-to-all-done.2
  77.3 3.9 %all-to-all-start = ((f32[16,32,512]{2,1,0:T(8,128)}), f32[16,32,512]{2,1,0:T(8,128)S(1)}, u32[]{:S(2)}, u32[]{:S(2)}) async-start(f32[16,32,512]{2,1,0:T(8,128)} %bitcast.54), calls=%async_computation | async-start | bytes 2097152 | tf_op jit(solution)/shard_map/all_to_all | solution.py:105
  81.2 0.1 sub.47
  81.3 0.8 reshape.123
  82.1 4.7 %convolution_convert_fusion = bf16[32,8192]{1,0:T(8,128)(2,1)} fusion(bf16[256,8192]{1,0:T(8,128)(2,1)} %param.15, bf16[32,4096]{1,0:T(8,128)(2,1)} %reshape.123, bf16[4096,256]{1,0:T(8,128)(2,1)S(1)} %copy-done, s32[256]{0:T(256)S(1)} %and_select_fusion.1, s32[32]{0:T(128)S(1)} %sub.47), kind=kOutput, calls=%fused_computation.4 | convolution fusion | flops 201613312 | bytes 7079040 | tf_op jit(solution)/shard_map/dot_general | solution.py:53
  86.8 2.2 %reshape.124 = bf16[16,2,8192]{2,1,0:T(2,128)(2,1)} reshape(bf16[32,8192]{1,0:T(8,128)(2,1)} %convolution_convert_fusion) | data formatting | bytes 1048576 | tf_op jit(solution)/shard_map/reshape | solution.py:56
  89.0 17.0 %all-to-all-done = f32[16,32,512]{2,1,0:T(8,128)S(1)} async-done(((f32[16,32,512]{2,1,0:T(8,128)}), f32[16,32,512]{2,1,0:T(8,128)S(1)}, u32[]{:S(2)}, u32[]{:S(2)}) %all-to-all-start) | async-done | bytes 1048608 | tf_op jit(solution)/shard_map/all_to_all | solution.py:105
  106.0 4.9 %all-to-all-start.3 = ((bf16[16,2,8192]{2,1,0:T(2,128)(2,1)}), bf16[16,2,8192]{2,1,0:T(2,128)(2,1)}, u32[]{:S(2)}, u32[]{:S(2)}) async-start(bf16[16,2,8192]{2,1,0:T(2,128)(2,1)} %reshape.124), calls=%async_computation.3 | async-start | bytes 1048576 | tf_op jit(solution)/shard_map/all_to_all | solution.py:60
  111.0 1.1 copy.34
  112.1 13.2 %all-to-all-done.3 = bf16[16,2,8192]{2,1,0:T(2,128)(2,1)} async-done(((bf16[16,2,8192]{2,1,0:T(2,128)(2,1)}), bf16[16,2,8192]{2,1,0:T(2,128)(2,1)}, u32[]{:S(2)}, u32[]{:S(2)}) %all-to-all-start.3) | async-done | bytes 524320 | tf_op jit(solution)/shard_map/all_to_all | solution.py:60
  125.2 2.6 %fusion.2 = bf16[32,8192]{1,0:T(8,128)(2,1)} fusion(f32[32,8192]{1,0:T(8,128)} %bitcast.53, bf16[16,2,8192]{2,1,0:T(2,128)(2,1)} %all-to-all-done.3, pred[2,32]{1,0:T(4,128)(4,1)S(1)} %iota_compare_fusion.3, pred[16,32]{1,0:T(8,128)(4,1)S(1)} %iota_compare_fusion.2), kind=kOutput, calls=%fused_computation.3 | convolution fusion | flops 17302528 | bytes 2097728 | tf_op jit(solution)/shard_map/ocr,ocd->rd/dot_general | solution.py:102
  (7 shorter events, 0.1 us)
Async XLA Ops:
  6.5 75.6 %copy-start = (bf16[4096,256]{1,0:T(8,128)(2,1)S(1)}, bf16[4096,256]{1,0:T(8,128)(2,1)}, u32[]{:S(2)}) copy-start(bf16[4096,256]{1,0:T(8,128)(2,1)} %param.14) | copy-start | bytes 6291460
  6.5 64.0 %all-gather.2.cloned.1.call-start = ((), (), s32[]{:S(2)}) async-start(), calls=%async_computation.4 | async-start | bytes 4456448 | tf_op jit(solution)/shard_map/all_gather | solution.py:98
  11.4 3.2 %copy-start.1 = (s32[32]{0:T(128)S(1)}, s32[32]{0:T(128)}, u32[]{:S(2)}) copy-start(s32[32]{0:T(128)} %param.12) | copy-start | bytes 388
  15.6 11.3 %all-to-all-start.1 = ((s32[16,1,2]{2,1,0:T(1,128)}), s32[16,1,2]{2,1,0:T(1,128)S(1)}, u32[]{:S(2)}, u32[]{:S(2)}) async-start(s32[16,1,2]{2,1,0:T(1,128)} %copy.29), calls=%async_computation.1 | async-start | bytes 16384 | tf_op jit(solution)/shard_map/all_to_all | solution.py:91
  26.9 50.4 %all-to-all-start.2 = ((bf16[16,2,4096]{2,1,0:T(2,128)(2,1)}), bf16[16,2,4096]{2,1,0:T(2,128)(2,1)S(1)}, u32[]{:S(2)}, u32[]{:S(2)}) async-start(bf16[16,2,4096]{2,1,0:T(2,128)(2,1)} %copy.30), calls=%async_computation.2 | async-start | bytes 524288 | tf_op jit(solution)/shard_map/all_to_all | solution.py:90
  77.3 28.8 %all-to-all-start = ((f32[16,32,512]{2,1,0:T(8,128)}), f32[16,32,512]{2,1,0:T(8,128)S(1)}, u32[]{:S(2)}, u32[]{:S(2)}) async-start(f32[16,32,512]{2,1,0:T(8,128)} %bitcast.54), calls=%async_computation | async-start | bytes 2097152 | tf_op jit(solution)/shard_map/all_to_all | solution.py:105
  106.0 19.2 %all-to-all-start.3 = ((bf16[16,2,8192]{2,1,0:T(2,128)(2,1)}), bf16[16,2,8192]{2,1,0:T(2,128)(2,1)}, u32[]{:S(2)}, u32[]{:S(2)}) async-start(bf16[16,2,8192]{2,1,0:T(2,128)(2,1)} %reshape.124), calls=%async_computation.3 | async-start | bytes 1048576 | tf_op jit(solution)/shard_map/all_to_all | solution.py:60
Sparse Core Ops, SparseCore 0:
  14.7 55.7 all-gather.1
where the time goes:
time: 136 us; the launch traced here: 135 us
  waiting for transfers between devices  72 us (53%)
  starting transfers between devices  20.7 us (15%)
  matrix products  19.6 us (14%)
  between operations  13.5 us (10%)
  local copies, waits for them, and re-layouts  7.75 us (6%)
    all_gather x1, waiting for transfers between devices, local(): lax.all_gather(attended, 'ad', axis=0, tiled=True)  38.4 us
    all_to_all x1, waiting for transfers between devices, local(): lax.all_to_all(base_cols, 'ad', split_axis=0, concat_axis=1, tiled=True)  17 us
    all_to_all x1, waiting for transfers between devices, send_back(): lax.all_to_all(delta_outputs, 'ad', split_axis=0, concat_axis=0, tiled=True)  13.2 us
    dot_general x1, matrix products, local(): jnp.dot(lax.all_gather(attended, 'ad', axis=0, tiled=True), output_weight...  6.76 us
    all_to_all x1, starting transfers between devices, local(): lax.all_to_all(send_ids, 'ad', split_axis=0, concat_axis=0, tiled=True)  6.61 us
    all_to_all x1, starting transfers between devices, local(): lax.all_to_all(send_rows, 'ad', split_axis=0, concat_axis=0, tiled=True)  5.23 us
    all_to_all x1, starting transfers between devices, send_back(): lax.all_to_all(delta_outputs, 'ad', split_axis=0, concat_axis=0, tiled=True)  4.94 us
    dot_general x1, matrix products, adapter_positions(): jnp.dot(reduced_rows, adapter_up_maps, preferred_element_type=jnp.float32)  4.72 us
  transfers between devices with their start and end apart: 5, of which 4 were waited for; matrix products, arithmetic and copies ran while one was open for 13% of the time, Pallas kernels for 0%

commit v1 on v0

v1 whole, which is shorter than its diff:
```python
import functools

import jax
import jax.numpy as jnp
from jax import lax
from jax.experimental import pallas as pl
from jax.experimental.pallas import tpu as pltpu
from jax.sharding import PartitionSpec as P

LOCAL_HEADS = 32
KV_HEADS = 4
HEAD_SIZE = 128
ADAPTER_RANK = 64
CAP = 2
FOLD = 8
PACK = FOLD * CAP
MESH = pl.DeviceIdType.MESH


def attend(queries, cached_key_vectors, stored_values, lengths):
    request_count, positions, kv_width = cached_key_vectors.shape
    group_size = LOCAL_HEADS // KV_HEADS
    query_heads = queries.reshape(request_count, KV_HEADS, group_size, HEAD_SIZE)
    key_heads = cached_key_vectors.reshape(request_count, positions, KV_HEADS, HEAD_SIZE)
    value_heads = stored_values.reshape(request_count, positions, KV_HEADS, HEAD_SIZE)
    scores = jnp.einsum(
        "rkgh,rckh->rkgc", query_heads, key_heads, preferred_element_type=jnp.float32
    ) * HEAD_SIZE ** (-0.5)
    live_mask = (jnp.arange(positions, dtype=jnp.int32)[None, :] < lengths[:, None])[
        :, None, None, :
    ]
    scores = jnp.where(live_mask, scores, jnp.float32(-1e30))
    row_max = jnp.max(scores, axis=-1, keepdims=True)
    exp_scores = jnp.where(live_mask, jnp.exp(scores - row_max), jnp.float32(0.0))
    probs = (exp_scores / jnp.sum(exp_scores, axis=-1, keepdims=True)).astype(jnp.bfloat16)
    attended = jnp.einsum("rkgc,rckh->rkgh", probs, value_heads, preferred_element_type=jnp.float32)
    return attended.reshape(request_count, LOCAL_HEADS * HEAD_SIZE).astype(jnp.bfloat16)


def iota(shape, axis):
    return lax.broadcasted_iota(jnp.int32, shape, axis)


def project_kernel(
    peers,
    snake,
    ids_row_ref,
    ids_col_ref,
    att_ref,
    w_hbm,
    down_hbm,
    up_hbm,
    out_ref,
    rows,
    w_ref,
    down_ref,
    up_ref,
    codes,
    base_send,
    base_recv,
    delta_send,
    delta_recv,
    load_sem,
    ring_send_sem,
    ring_recv_sem,
    sib_send_sem,
    sib_recv_sem,
    code_send_sem,
    code_recv_sem,
    base_send_sem,
    base_recv_sem,
    delta_send_sem,
    delta_recv_sem,
):
    own_rows, width = att_ref.shape
    half = own_rows // 2
    chips = peers // 2
    hops = chips // 2
    columns = w_ref.shape[1]
    share = down_ref.shape[1] // ADAPTER_RANK
    fold_width = up_ref.shape[1] // FOLD

    loads = [
        pltpu.make_async_copy(src, dst, load_sem.at[i])
        for i, (src, dst) in enumerate(((w_hbm, w_ref), (down_hbm, down_ref), (up_hbm, up_ref)))
    ]
    for load in loads:
        load.start()

    me = lax.axis_index("ad")
    core = lax.rem(me, 2)
    my_chip = me // 2

    def place(chip):
        if not snake:
            return chip
        side = lax.rem(chip, 2)
        return (1 - side) * (chip // 2) + side * (chips - 1 - chip // 2)

    def chip_at(spot):
        spot = lax.rem(spot + 2 * chips, chips)
        if not snake:
            return spot
        side = spot // hops
        return (1 - side) * (2 * spot) + side * (2 * chips - 1 - 2 * spot)

    spot = place(my_chip)
    right = chip_at(spot + 1) * 2 + core
    left = chip_at(spot - 1) * 2 + core
    sibling = my_chip * 2 + 1 - core

    barrier = pltpu.get_barrier_semaphore()

    def greet(step, carry):
        pl.semaphore_signal(
            barrier, inc=1, device_id={"ad": lax.rem(me + step, peers)}, device_id_type=MESH
        )
        return carry

    lax.fori_loop(1, peers, greet, 0)

    ids_row = ids_row_ref[...]
    ids_col = ids_col_ref[...]
    owner_row = ids_row // share
    owner_col = ids_col // share
    same = owner_row == owner_col
    first = iota((own_rows, own_rows), 0)
    second = iota((own_rows, own_rows), 1)
    rank_row = jnp.sum((same & (first < second)).astype(jnp.int32), axis=0, keepdims=True)
    rank_col = jnp.sum((same & (second < first)).astype(jnp.int32), axis=1, keepdims=True)
    slot_col = owner_col * CAP + rank_col
    code_row = (owner_row * CAP + rank_row - owner_row) * share + ids_row
    my_codes = codes.at[pl.ds(pl.multiple_of(me * 8, 8), 8)]
    my_codes[:, :own_rows] = jnp.broadcast_to(code_row, (8, own_rows))
    my_codes[:, own_rows:] = jnp.zeros((8, 128 - own_rows), jnp.int32)
    rows[pl.ds(pl.multiple_of(me * own_rows, own_rows), own_rows), :] = att_ref[...]

    pl.semaphore_wait(barrier, peers - 1)

    def ring_copy(direction, hop, part):
        back = hop - 1
        source = chip_at(spot - back if direction == 0 else spot + back) * 2 + core
        piece = rows.at[pl.ds(pl.multiple_of(source * own_rows + part * half, half), half)]
        index = ((hop - 1) * 2 + direction) * 2 + part
        return pltpu.make_async_remote_copy(
            src_ref=piece,
            dst_ref=piece,
            send_sem=ring_send_sem.at[index],
            recv_sem=ring_recv_sem.at[index],
            device_id={"ad": right if direction == 0 else left},
            device_id_type=MESH,
        )

    def ring_arrival(direction, hop, part):
        source = chip_at(spot - hop if direction == 0 else spot + hop) * 2 + core
        piece = rows.at[pl.ds(pl.multiple_of(source * own_rows + part * half, half), half)]
        index = ((hop - 1) * 2 + direction) * 2 + part
        return pltpu.make_async_remote_copy(
            src_ref=piece,
            dst_ref=piece,
            send_sem=ring_send_sem.at[index],
            recv_sem=ring_recv_sem.at[index],
            device_id={"ad": right if direction == 0 else left},
            device_id_type=MESH,
        )

    def sib_copy(direction, hop, part, their_core):
        source = chip_at(spot - hop if direction == 0 else spot + hop) * 2 + their_core
        piece = rows.at[pl.ds(pl.multiple_of(source * own_rows + part * half, half), half)]
        index = (hop * 2 + direction) * 2 + part
        return pltpu.make_async_remote_copy(
            src_ref=piece,
            dst_ref=piece,
            send_sem=sib_send_sem.at[index],
            recv_sem=sib_recv_sem.at[index],
            device_id={"ad": sibling},
            device_id_type=MESH,
        )

    for part in range(2):
        ring_copy(0, 1, part).start()
        ring_copy(1, 1, part).start()
        sib_copy(0, 0, part, core).start()

    def code_copy(source, target):
        piece = codes.at[pl.ds(pl.multiple_of(source * 8, 8), 8)]
        return pltpu.make_async_remote_copy(
            src_ref=piece,
            dst_ref=piece,
            send_sem=code_send_sem.at[target],
            recv_sem=code_recv_sem.at[source],
            device_id={"ad": target},
            device_id_type=MESH,
        )

    def send_codes(step, carry):
        code_copy(me, lax.rem(me + step, peers)).start()
        return carry

    lax.fori_loop(1, peers, send_codes, 0)

    def base_copy(source, target):
        return pltpu.make_async_remote_copy(
            src_ref=base_send.at[target],
            dst_ref=base_recv.at[source],
            send_sem=base_send_sem.at[target],
            recv_sem=base_recv_sem.at[source],
            device_id={"ad": target},
            device_id_type=MESH,
        )

    def delta_copy(source, target):
        return pltpu.make_async_remote_copy(
            src_ref=delta_send.at[pl.ds(pl.multiple_of(target * PACK, PACK), PACK)],
            dst_ref=delta_recv.at[pl.ds(pl.multiple_of(source * PACK, PACK), PACK)],
            send_sem=delta_send_sem.at[target],
            recv_sem=delta_recv_sem.at[source],
            device_id={"ad": target},
            device_id_type=MESH,
        )

    for load in loads:
        load.wait()

    def each_piece(hop, action):
        for part in range(2):
            for direction in range(2):
                if part == direction:
                    action(direction, part)
                else:
                    pl.when(hop < hops)(functools.partial(action, direction, part))

    def step(hop, carry):
        def arrive(direction, part):
            ring_arrival(direction, hop, part).wait_recv()
            if part == direction:
                pl.when(hop < hops)(lambda: ring_copy(direction, hop + 1, part).start())
            else:
                pl.when(hop < hops - 1)(lambda: ring_copy(direction, hop + 1, part).start())
            sib_copy(direction, hop, part, core).start()

        each_piece(hop, arrive)
        each_piece(hop, lambda d, p: sib_copy(d, hop, p, 1 - core).wait_recv())

        @pl.when(hop == hops)
        def _():
            for part in range(2):
                sib_copy(0, 0, part, 1 - core).wait_recv()

        low = chip_at(spot - lax.rem(hop, hops))
        high = chip_at(spot + hop)
        block = jnp.concatenate(
            [
                rows[pl.ds(pl.multiple_of(chip * 2 * own_rows, 2 * own_rows), 2 * own_rows), :]
                for chip in (low, high)
            ],
            axis=0,
        )
        devices = [low * 2, low * 2 + 1, high * 2, high * 2 + 1]
        shrunk = jnp.dot(block, down_ref[...], preferred_element_type=jnp.float32).astype(
            jnp.bfloat16
        )
        picked = []
        for i, device in enumerate(devices):
            pl.when(device != me)(lambda device=device: code_copy(device, me).wait_recv())
            code = codes[pl.ds(pl.multiple_of(device * 8, 8), 8), :own_rows][:1]
            floor = (me * CAP + lax.rem(iota((PACK, own_rows), 0), CAP)) * share
            pick = (code >= floor) & (code < floor + share)
            local_id = jnp.sum(jnp.where(pick, code - floor, 0), axis=1, keepdims=True)
            chosen = jnp.dot(
                pick.astype(jnp.bfloat16),
                shrunk[i * own_rows : (i + 1) * own_rows],
                preferred_element_type=jnp.float32,
            )
            lane = iota(chosen.shape, 1)
            mine = (lane >= local_id * ADAPTER_RANK) & (lane < (local_id + 1) * ADAPTER_RANK)
            picked.append(jnp.where(mine, chosen, 0.0))
        picked = jnp.concatenate(picked, axis=0)
        fold_of = lax.rem(iota(picked.shape, 0), PACK) // CAP
        total = None
        for fold in range(FOLD):
            term = jnp.dot(
                jnp.where(fold_of == fold, picked, 0.0).astype(jnp.bfloat16),
                up_ref[:, fold * fold_width : (fold + 1) * fold_width],
                preferred_element_type=jnp.float32,
            )
            total = term if total is None else total + term
        total = total.astype(jnp.bfloat16)
        for i, device in enumerate(devices):
            piece = total[i * PACK : (i + 1) * PACK]

            @pl.when(device != me)
            def _():
                delta_send[pl.ds(pl.multiple_of(device * PACK, PACK), PACK), :] = piece
                delta_copy(me, device).start()

            @pl.when(device == me)
            def _():
                delta_recv[pl.ds(pl.multiple_of(device * PACK, PACK), PACK), :] = piece

        base = jnp.dot(block, w_ref[...], preferred_element_type=jnp.float32).astype(jnp.bfloat16)
        for i, device in enumerate(devices):
            piece = base[i * own_rows : (i + 1) * own_rows]

            @pl.when(device != me)
            def _():
                base_send[device] = piece
                base_copy(me, device).start()

            @pl.when(device == me)
            def _():
                base_recv[device] = piece

        return carry

    lax.fori_loop(1, hops + 1, step, 0)

    def collect(offset, carry):
        device = lax.rem(me + offset, peers)
        delta_copy(device, me).wait_recv()
        base_copy(device, me).wait_recv()
        return carry

    lax.fori_loop(1, peers, collect, 0)

    lane = iota((own_rows, peers * PACK), 1)
    lane_slot = (lane // PACK) * CAP + lax.rem(lane, CAP)
    lane_fold = lax.rem(lane, PACK) // CAP
    here = lane_slot == slot_col
    take = jnp.concatenate(
        [(here & (lane_fold == fold)).astype(jnp.bfloat16) for fold in range(FOLD)], axis=0
    )
    deltas = jnp.dot(take, delta_recv[...], preferred_element_type=jnp.float32)
    for device in range(peers):
        fold, start = divmod(device * columns, fold_width)
        out_ref[:, device * columns : (device + 1) * columns] = (
            base_recv[device].astype(jnp.float32)
            + deltas[fold * own_rows : (fold + 1) * own_rows, start : start + columns]
        ).astype(jnp.bfloat16)

    def finish(offset, carry):
        device = lax.rem(me + offset, peers)
        code_copy(me, device).wait_send()
        delta_copy(me, device).wait_send()
        base_copy(me, device).wait_send()
        return carry

    lax.fori_loop(1, peers, finish, 0)

    for part in range(2):
        sib_copy(0, 0, part, core).wait_send()

    def drain(hop, carry):
        def one(direction, part):
            ring_copy(direction, hop, part).wait_send()
            sib_copy(direction, hop, part, core).wait_send()

        each_piece(hop, one)
        return carry

    lax.fori_loop(1, hops + 1, drain, 0)


def project(ids, attended, weights, down, up, snake):
    peers = lax.axis_size("ad")
    own_rows, width = attended.shape
    columns = weights.shape[1]
    hops = peers // 4
    model_width = up.shape[1]
    vmem = pl.BlockSpec(memory_space=pltpu.VMEM)
    hbm = pl.BlockSpec(memory_space=pl.ANY)
    dma = pltpu.SemaphoreType.DMA
    return pl.pallas_call(
        functools.partial(project_kernel, peers, snake),
        out_shape=jax.ShapeDtypeStruct((own_rows, model_width), jnp.bfloat16),
        in_specs=[vmem, vmem, vmem, hbm, hbm, hbm],
        out_specs=vmem,
        scratch_shapes=[
            pltpu.VMEM((peers * own_rows, width), jnp.bfloat16),
            pltpu.VMEM(weights.shape, jnp.bfloat16),
            pltpu.VMEM(down.shape, jnp.bfloat16),
            pltpu.VMEM(up.shape, jnp.bfloat16),
            pltpu.VMEM((peers * 8, 128), jnp.int32),
            pltpu.VMEM((peers, own_rows, columns), jnp.bfloat16),
            pltpu.VMEM((peers, own_rows, columns), jnp.bfloat16),
            pltpu.VMEM((peers * PACK, model_width // FOLD), jnp.bfloat16),
            pltpu.VMEM((peers * PACK, model_width // FOLD), jnp.bfloat16),
            dma((3,)),
            dma((hops * 4,)),
            dma((hops * 4,)),
            dma(((hops + 1) * 4,)),
            dma(((hops + 1) * 4,)),
            dma((peers,)),
            dma((peers,)),
            dma((peers,)),
            dma((peers,)),
            dma((peers,)),
            dma((peers,)),
        ],
        compiler_params=pltpu.CompilerParams(
            collective_id=0, has_side_effects=True, vmem_limit_bytes=56 * 1024 * 1024
        ),
        cost_estimate=pl.CostEstimate(
            flops=2 * peers * own_rows * width * (columns + down.shape[1]),
            bytes_accessed=2 * (weights.size + down.size + up.size),
            transcendentals=0,
        ),
    )(ids.reshape(1, own_rows), ids.reshape(own_rows, 1), attended, weights, down, up)


def local(
    snake,
    queries,
    cached_key_vectors,
    stored_values,
    lengths,
    request_adapters,
    output_weight_rows,
    adapter_down_maps,
    adapter_up_maps,
):
    attended = attend(queries, cached_key_vectors, stored_values, lengths)
    return project(
        request_adapters,
        attended,
        output_weight_rows,
        adapter_down_maps,
        adapter_up_maps,
        snake,
    )


def solution(mesh):
    return jax.shard_map(
        functools.partial(local, mesh.shape["ad"] == 16),
        mesh=mesh,
        in_specs=(
            P(("grp", "ad"), None),
            P(("grp", "ad"), None, None),
            P(("grp", "ad"), None, None),
            P(("grp", "ad")),
            P(("grp", "ad")),
            P(None, "ad"),
            P(None, "ad"),
            P("ad", None),
        ),
        out_specs=P(("grp", "ad"), None),
        check_vma=False,
    )
```

time: 136 us -> 64.5 us (0.47)
  the two profiles are of different devices: /device:TPU:9 before, /device:TPU:17 now
where the time goes in v1:
time: 64.5 us; the launch traced here: 64.2 us
  Pallas kernels  54.6 us (85%)
  local copies, waits for them, and re-layouts  5.01 us (8%)
  matrix products  3.7 us (6%)
  other arithmetic  0.88 us (1%)
    pallas_call x1, Pallas kernels, project(): pl.pallas_call(functools.partial(project_kernel, peers, snake), out_shape...  54.6 us
    unnamed x5, local copies, waits for them, and re-layouts  3.68 us
    sub x1, matrix products, attend(): scores - row_max  2.97 us
    reshape x1, local copies, waits for them, and re-layouts, project(): ids.reshape(own_rows, 1)  1.33 us

profile of v1, /device:TPU:17, one launch (start us, length us, event | category | flops | bytes accessed | tf_op | source)
XLA Modules:
  0.0 64.2 jit_solution(12946798668489893809)
XLA Ops:
  0.0 0.0 copy-start
  0.0 0.9 %iota_compare_fusion = pred[32,64]{1,0:T(8,128)(4,1)S(1)} fusion(s32[32]{0:T(128)} %param.11), kind=kLoop, calls=%fused_computation.16 | loop fusion | flops 2048 | bytes 2176 | tf_op jit(solution)/shard_map/lt | solution.py:29
  0.9 1.3 %copy.11.ids_col_ref = s32[32,1]{1,0:T(8,128)} copy(s32[32,1]{0,1:T(1,128)} %bitcast.38) | data formatting | bytes 256 | tf_op jit(solution)/shard_map/reshape | solution.py:408
  2.2 1.0 %copy.14 = bf16[4,8,32,128]{3,2,1,0:T(8,128)(2,1)S(1)} copy(bf16[4,8,32,128]{3,1,2,0:T(8,128)(2,1)} %bitcast.34) | data formatting | bytes 524288
  3.2 3.0 %fusion.20 = (f32[32,4,8]{2,1,0:T(4,128)S(1)}, f32[32,4,8,64]{3,2,1,0:T(8,128)S(1)}) fusion(pred[32,64]{1,0:T(8,128)(4,1)S(1)} %iota_compare_fusion, bf16[32,4,8,128]{3,2,1,0:T(8,128)(2,1)S(1)} %bitcast.35, bf16[32,64,512]{2,1,0:T(8,128)(2,1)} %param.9), kind=kOutput, calls=%fused_computation.17 | convolution fusion | flops 17104960 | bytes 2627584 | tf_op jit(solution)/shard_map/sub | solution.py:34
  6.2 0.0 copy-done
  6.2 0.7 %fusion.16 = bf16[32,4,8,128]{3,2,1,0:T(8,128)(2,1)S(1)} fusion(f32[32,4,8,64]{3,2,1,0:T(8,128)S(1)} %get-tuple-element.6, f32[32,4,8]{2,1,0:T(4,128)S(1)} %get-tuple-element.5, bf16[32,64,512]{2,1,0:T(8,128)(2,1)S(1)} %copy-done), kind=kOutput, calls=%fused_computation.12 | convolution fusion | flops 17039360 | bytes 2625536 | tf_op jit(solution)/shard_map/rkgc,rckh->rkgh/dot_general | solution.py:36
  6.9 0.8 %copy.33 = bf16[4,8,32,128]{3,1,2,0:T(8,128)(2,1)} copy(bf16[4,8,32,128]{3,2,1,0:T(8,128)(2,1)S(1)} %bitcast.36) | data formatting | bytes 524288
  7.7 54.6 %shard_map.82 = bf16[32,8192]{1,0:T(8,128)(2,1)} custom-call(s32[1,32]{1,0:T(1,128)} %bitcast.39, s32[32,1]{1,0:T(8,128)} %copy.11.ids_col_ref, bf16[32,4096]{1,0:T(8,128)(2,1)} %bitcast.37, bf16[4096,512]{1,0:T(8,128)(2,1)} %w_hbm.1, bf16[4096,256]{1,0:T(8,128)(2,1)} %down_hbm.1, bf16[256,8192]{1,0:T(8,128)(2,1)} %up_hbm.1), custom_call_target="tpu_custom_call" | custom-call | flops 3221225472 | bytes 10485760 | tf_op jit(solution)/shard_map/pallas_call | solution.py:373
  62.4 1.9 %copy.35 = bf16[32,8192]{1,0:T(8,128)(2,1)} copy(bf16[32,8192]{1,0:T(8,128)(2,1)} %shard_map.82) | data formatting | bytes 1048576
Async XLA Ops:
  0.0 6.2 %copy-start = (bf16[32,64,512]{2,1,0:T(8,128)(2,1)S(1)}, bf16[32,64,512]{2,1,0:T(8,128)(2,1)}, u32[]{:S(2)}) copy-start(bf16[32,64,512]{2,1,0:T(8,128)(2,1)} %param.10) | copy-start | bytes 6291460

commit v2 on v1

--- a/solution.py
+++ b/solution.py
@@ -17,28 +17,62 @@
 MESH = pl.DeviceIdType.MESH
 
 
-def attend(queries, cached_key_vectors, stored_values, lengths):
-    request_count, positions, kv_width = cached_key_vectors.shape
-    group_size = LOCAL_HEADS // KV_HEADS
-    query_heads = queries.reshape(request_count, KV_HEADS, group_size, HEAD_SIZE)
-    key_heads = cached_key_vectors.reshape(request_count, positions, KV_HEADS, HEAD_SIZE)
-    value_heads = stored_values.reshape(request_count, positions, KV_HEADS, HEAD_SIZE)
-    scores = jnp.einsum(
-        "rkgh,rckh->rkgc", query_heads, key_heads, preferred_element_type=jnp.float32
-    ) * HEAD_SIZE ** (-0.5)
-    live_mask = (jnp.arange(positions, dtype=jnp.int32)[None, :] < lengths[:, None])[
-        :, None, None, :
-    ]
-    scores = jnp.where(live_mask, scores, jnp.float32(-1e30))
-    row_max = jnp.max(scores, axis=-1, keepdims=True)
-    exp_scores = jnp.where(live_mask, jnp.exp(scores - row_max), jnp.float32(0.0))
-    probs = (exp_scores / jnp.sum(exp_scores, axis=-1, keepdims=True)).astype(jnp.bfloat16)
-    attended = jnp.einsum("rkgc,rckh->rkgh", probs, value_heads, preferred_element_type=jnp.float32)
-    return attended.reshape(request_count, LOCAL_HEADS * HEAD_SIZE).astype(jnp.bfloat16)
-
-
 def iota(shape, axis):
     return lax.broadcasted_iota(jnp.int32, shape, axis)
+
+
+def attend(first, count, lengths_ref, queries_ref, keys, values, heads, out_rows):
+    positions, kv_width = keys.shape[1:]
+    group_size = LOCAL_HEADS // KV_HEADS
+    for head in range(LOCAL_HEADS):
+        heads[pl.ds(head, count, stride=LOCAL_HEADS), :] = queries_ref[
+            first : first + count, head * HEAD_SIZE : (head + 1) * HEAD_SIZE
+        ].astype(jnp.float32)
+    batch = 8
+    shape = (LOCAL_HEADS, kv_width)
+    own_group = iota(shape, 0) // group_size == iota(shape, 1) // HEAD_SIZE
+
+    def some(turn, carry):
+        scores, live = [], []
+        for i in range(batch):
+            place = turn * batch + i
+            query = heads[pl.ds(pl.multiple_of(place * LOCAL_HEADS, LOCAL_HEADS), LOCAL_HEADS), :]
+            wide = jnp.where(own_group, jnp.concatenate([query] * KV_HEADS, axis=1), 0.0)
+            scores.append(
+                lax.dot_general(
+                    wide.astype(jnp.bfloat16),
+                    keys[first + place],
+                    (((1,), (1,)), ((), ())),
+                    preferred_element_type=jnp.float32,
+                )
+            )
+            live.append(iota((LOCAL_HEADS, positions), 1) < lengths_ref[first + place])
+        for i in range(batch):
+            place = turn * batch + i
+            score = jnp.where(live[i], scores[i] * HEAD_SIZE ** (-0.5), jnp.float32(-1e30))
+            row_max = jnp.max(score, axis=-1, keepdims=True)
+            weight = jnp.where(live[i], jnp.exp(score - row_max), 0.0)
+            probs = (weight / jnp.sum(weight, axis=-1, keepdims=True)).astype(jnp.bfloat16)
+            mixed = jnp.dot(probs, values[first + place], preferred_element_type=jnp.float32)
+            heads[pl.ds(pl.multiple_of(place * LOCAL_HEADS, LOCAL_HEADS), LOCAL_HEADS), :] = (
+                jnp.concatenate(
+                    [
+                        mixed[
+                            g * group_size : (g + 1) * group_size,
+                            g * HEAD_SIZE : (g + 1) * HEAD_SIZE,
+                        ]
+                        for g in range(KV_HEADS)
+                    ],
+                    axis=0,
+                )
+            )
+        return carry
+
+    lax.fori_loop(0, count // batch, some, 0)
+    for head in range(LOCAL_HEADS):
+        out_rows[:, head * HEAD_SIZE : (head + 1) * HEAD_SIZE] = heads[
+            pl.ds(head, count, stride=LOCAL_HEADS), :
+        ].astype(jnp.bfloat16)
 
 
 def project_kernel(
@@ -46,12 +80,18 @@
     snake,
     ids_row_ref,
     ids_col_ref,
-    att_ref,
+    lengths_ref,
+    queries_ref,
+    keys_hbm,
+    values_hbm,
     w_hbm,
     down_hbm,
     up_hbm,
     out_ref,
     rows,
+    heads,
+    keys,
+    values,
     w_ref,
     down_ref,
     up_ref,
@@ -72,7 +112,7 @@
     delta_send_sem,
     delta_recv_sem,
 ):
-    own_rows, width = att_ref.shape
+    own_rows, width = queries_ref.shape
     half = own_rows // 2
     chips = peers // 2
     hops = chips // 2
@@ -84,7 +124,16 @@
         pltpu.make_async_copy(src, dst, load_sem.at[i])
         for i, (src, dst) in enumerate(((w_hbm, w_ref), (down_hbm, down_ref), (up_hbm, up_ref)))
     ]
-    for load in loads:
+    cache_loads = [
+        pltpu.make_async_copy(
+            src.at[pl.ds(part * half, half)],
+            dst.at[pl.ds(part * half, half)],
+            load_sem.at[3 + part * 2 + i],
+        )
+        for part in range(2)
+        for i, (src, dst) in enumerate(((keys_hbm, keys), (values_hbm, values)))
+    ]
+    for load in cache_loads + loads:
         load.start()
 
     me = lax.axis_index("ad")
@@ -133,9 +182,6 @@
     my_codes = codes.at[pl.ds(pl.multiple_of(me * 8, 8), 8)]
     my_codes[:, :own_rows] = jnp.broadcast_to(code_row, (8, own_rows))
     my_codes[:, own_rows:] = jnp.zeros((8, 128 - own_rows), jnp.int32)
-    rows[pl.ds(pl.multiple_of(me * own_rows, own_rows), own_rows), :] = att_ref[...]
-
-    pl.semaphore_wait(barrier, peers - 1)
 
     def ring_copy(direction, hop, part):
         back = hop - 1
@@ -178,6 +224,15 @@
         )
 
     for part in range(2):
+        for load in cache_loads[part * 2 : part * 2 + 2]:
+            load.wait()
+        start = pl.multiple_of(me * own_rows + part * half, half)
+        attend(
+            part * half, half, lengths_ref, queries_ref, keys, values, heads,
+            rows.at[pl.ds(start, half)],
+        )
+        if part == 0:
+            pl.semaphore_wait(barrier, peers - 1)
         ring_copy(0, 1, part).start()
         ring_copy(1, 1, part).start()
         sib_copy(0, 0, part, core).start()
@@ -361,22 +416,26 @@
     lax.fori_loop(1, hops + 1, drain, 0)
 
 
-def project(ids, attended, weights, down, up, snake):
+def project(ids, lengths, queries, keys, values, weights, down, up, snake):
     peers = lax.axis_size("ad")
-    own_rows, width = attended.shape
+    own_rows, width = queries.shape
     columns = weights.shape[1]
     hops = peers // 4
     model_width = up.shape[1]
     vmem = pl.BlockSpec(memory_space=pltpu.VMEM)
+    smem = pl.BlockSpec(memory_space=pltpu.SMEM)
     hbm = pl.BlockSpec(memory_space=pl.ANY)
     dma = pltpu.SemaphoreType.DMA
     return pl.pallas_call(
         functools.partial(project_kernel, peers, snake),
         out_shape=jax.ShapeDtypeStruct((own_rows, model_width), jnp.bfloat16),
-        in_specs=[vmem, vmem, vmem, hbm, hbm, hbm],
+        in_specs=[vmem, vmem, smem, vmem, hbm, hbm, hbm, hbm, hbm],
         out_specs=vmem,
         scratch_shapes=[
             pltpu.VMEM((peers * own_rows, width), jnp.bfloat16),
+            pltpu.VMEM((own_rows // 2 * LOCAL_HEADS, HEAD_SIZE), jnp.float32),
+            pltpu.VMEM(keys.shape, jnp.bfloat16),
+            pltpu.VMEM(values.shape, jnp.bfloat16),
             pltpu.VMEM(weights.shape, jnp.bfloat16),
             pltpu.VMEM(down.shape, jnp.bfloat16),
             pltpu.VMEM(up.shape, jnp.bfloat16),
@@ -385,7 +444,7 @@
             pltpu.VMEM((peers, own_rows, columns), jnp.bfloat16),
             pltpu.VMEM((peers * PACK, model_width // FOLD), jnp.bfloat16),
             pltpu.VMEM((peers * PACK, model_width // FOLD), jnp.bfloat16),
-            dma((3,)),
+            dma((7,)),
             dma((hops * 4,)),
             dma((hops * 4,)),
             dma(((hops + 1) * 4,)),
@@ -405,7 +464,7 @@
             bytes_accessed=2 * (weights.size + down.size + up.size),
             transcendentals=0,
         ),
-    )(ids.reshape(1, own_rows), ids.reshape(own_rows, 1), attended, weights, down, up)
+    )(ids.reshape(1, own_rows), ids.reshape(own_rows, 1), lengths, queries, keys, values, weights, down, up)
 
 
 def local(
@@ -419,10 +478,12 @@
     adapter_down_maps,
     adapter_up_maps,
 ):
-    attended = attend(queries, cached_key_vectors, stored_values, lengths)
     return project(
         request_adapters,
-        attended,
+        lengths,
+        queries,
+        cached_key_vectors,
+        stored_values,
         output_weight_rows,
         adapter_down_maps,
         adapter_up_maps,

time: 64.5 us -> 57.3 us (0.89)
  the two profiles are of different devices: /device:TPU:17 before, /device:TPU:9 now
where the time goes in v2:
time: 57.3 us; the launch traced here: 57.1 us
  Pallas kernels  53.9 us (94%)
  local copies, waits for them, and re-layouts  3.21 us (6%)
    pallas_call x1, Pallas kernels, project(): pl.pallas_call(functools.partial(project_kernel, peers, snake), out_shape...  53.9 us
    unnamed x1, local copies, waits for them, and re-layouts  1.87 us
    reshape x1, local copies, waits for them, and re-layouts, project(): ids.reshape(own_rows, 1)  1.34 us

profile of v2, /device:TPU:9, one launch (start us, length us, event | category | flops | bytes accessed | tf_op | source)
XLA Modules:
  0.0 57.1 jit_solution(13170119489639630657)
XLA Ops:
  0.0 1.3 %copy.9.ids_col_ref = s32[32,1]{1,0:T(8,128)} copy(s32[32,1]{0,1:T(1,128)} %bitcast.2) | data formatting | bytes 256 | tf_op jit(solution)/shard_map/reshape | solution.py:467
  1.3 53.9 %shard_map.82 = bf16[32,8192]{1,0:T(8,128)(2,1)} custom-call(s32[1,32]{1,0:T(1,128)} %bitcast.3, s32[32,1]{1,0:T(8,128)} %copy.9.ids_col_ref, s32[32]{0:T(128)} %lengths_ref.1, bf16[32,4096]{1,0:T(8,128)(2,1)} %queries_ref.1, bf16[32,64,512]{2,1,0:T(8,128)(2,1)} %keys_hbm.1, bf16[32,64,512]{2,1,0:T(8,128)(2,1)} %values_hbm.1, bf16[4096,512]{1,0:T(8,128)(2,1)} %w_hbm.1, ...), custom_call_target="tpu_custom_call" | custom-call | flops 3221225472 | bytes 10485760 | tf_op jit(solution)/shard_map/pallas_call | solution.py:429
  55.2 1.9 %copy.11 = bf16[32,8192]{1,0:T(8,128)(2,1)} copy(bf16[32,8192]{1,0:T(8,128)(2,1)} %shard_map.82) | data formatting | bytes 1048576

commit v3 on v2

--- a/solution.py
+++ b/solution.py
@@ -77,9 +77,8 @@
 
 def project_kernel(
     peers,
-    snake,
+    block_2x4,
     ids_row_ref,
-    ids_col_ref,
     lengths_ref,
     queries_ref,
     keys_hbm,
@@ -140,20 +139,10 @@
     core = lax.rem(me, 2)
     my_chip = me // 2
 
-    def place(chip):
-        if not snake:
-            return chip
-        side = lax.rem(chip, 2)
-        return (1 - side) * (chip // 2) + side * (chips - 1 - chip // 2)
-
     def chip_at(spot):
-        spot = lax.rem(spot + 2 * chips, chips)
-        if not snake:
-            return spot
-        side = spot // hops
-        return (1 - side) * (2 * spot) + side * (2 * chips - 1 - 2 * spot)
-
-    spot = place(my_chip)
+        return lax.rem(spot + 2 * chips, chips)
+
+    spot = my_chip
     right = chip_at(spot + 1) * 2 + core
     left = chip_at(spot - 1) * 2 + core
     sibling = my_chip * 2 + 1 - core
@@ -169,12 +158,11 @@
     lax.fori_loop(1, peers, greet, 0)
 
     ids_row = ids_row_ref[...]
-    ids_col = ids_col_ref[...]
     owner_row = ids_row // share
-    owner_col = ids_col // share
-    same = owner_row == owner_col
     first = iota((own_rows, own_rows), 0)
     second = iota((own_rows, own_rows), 1)
+    owner_col = jnp.sum(jnp.where(first == second, owner_row, 0), axis=1, keepdims=True)
+    same = owner_row == owner_col
     rank_row = jnp.sum((same & (first < second)).astype(jnp.int32), axis=0, keepdims=True)
     rank_col = jnp.sum((same & (second < first)).astype(jnp.int32), axis=1, keepdims=True)
     slot_col = owner_col * CAP + rank_col
@@ -223,6 +211,69 @@
             device_id_type=MESH,
         )
 
+    side = lax.rem(my_chip, 2)
+    level = my_chip // 2
+    last = chips // 2 - 1
+    upper = level // 2
+    middle = level * (last - level) // 2
+
+    def nearest(turn):
+        near = upper * (last - level) + (1 - upper) * level
+        near = turn + near * (1 - 2 * turn) * (1 - turn // 2)
+        return upper * (last - near) + (1 - upper) * near
+
+    def piece_of(chip, its_core, part):
+        start = (chip * 2 + its_core) * own_rows + part * half
+        return rows.at[pl.ds(pl.multiple_of(start, half), half)]
+
+    def z_copy(source, up, part):
+        piece = piece_of(source * 2 + side, core, part)
+        there = lax.rem(level + 1 if up else level + last, last + 1)
+        return pltpu.make_async_remote_copy(
+            src_ref=piece,
+            dst_ref=piece,
+            send_sem=ring_send_sem.at[(source + (last + 1 if up else 0)) * 2 + part],
+            recv_sem=ring_recv_sem.at[source * 2 + part],
+            device_id={"ad": (there * 2 + side) * 2 + core},
+            device_id_type=MESH,
+        )
+
+    def y_copy(source, its_side, part):
+        piece = piece_of(source * 2 + its_side, core, part)
+        return pltpu.make_async_remote_copy(
+            src_ref=piece,
+            dst_ref=piece,
+            send_sem=ring_send_sem.at[(source + 2 * (last + 1)) * 2 + part],
+            recv_sem=ring_recv_sem.at[(source + last + 1) * 2 + part],
+            device_id={"ad": (level * 2 + 1 - side) * 2 + core},
+            device_id_type=MESH,
+        )
+
+    def twin_copy(chip, part, its_core):
+        piece = piece_of(chip, its_core, part)
+        return pltpu.make_async_remote_copy(
+            src_ref=piece,
+            dst_ref=piece,
+            send_sem=sib_send_sem.at[chip * 2 + part],
+            recv_sem=sib_recv_sem.at[chip * 2 + part],
+            device_id={"ad": sibling},
+            device_id_type=MESH,
+        )
+
+    def z_sends(source, part, action):
+        @pl.when((source <= level) & (level < last))
+        def _():
+            action(z_copy(source, True, part))
+
+        @pl.when((source >= level) & (level > 0))
+        def _():
+            action(z_copy(source, False, part))
+
+    def pass_on(source, part):
+        z_sends(source, part, lambda copy: copy.start())
+        y_copy(source, side, part).start()
+        twin_copy(source * 2 + side, part, core).start()
+
     for part in range(2):
         for load in cache_loads[part * 2 : part * 2 + 2]:
             load.wait()
@@ -233,9 +284,12 @@
         )
         if part == 0:
             pl.semaphore_wait(barrier, peers - 1)
-        ring_copy(0, 1, part).start()
-        ring_copy(1, 1, part).start()
-        sib_copy(0, 0, part, core).start()
+        if block_2x4:
+            pass_on(level, part)
+        else:
+            ring_copy(0, 1, part).start()
+            ring_copy(1, 1, part).start()
+            sib_copy(0, 0, part, core).start()
 
     def code_copy(source, target):
         piece = codes.at[pl.ds(pl.multiple_of(source * 8, 8), 8)]
@@ -285,25 +339,7 @@
                 else:
                     pl.when(hop < hops)(functools.partial(action, direction, part))
 
-    def step(hop, carry):
-        def arrive(direction, part):
-            ring_arrival(direction, hop, part).wait_recv()
-            if part == direction:
-                pl.when(hop < hops)(lambda: ring_copy(direction, hop + 1, part).start())
-            else:
-                pl.when(hop < hops - 1)(lambda: ring_copy(direction, hop + 1, part).start())
-            sib_copy(direction, hop, part, core).start()
-
-        each_piece(hop, arrive)
-        each_piece(hop, lambda d, p: sib_copy(d, hop, p, 1 - core).wait_recv())
-
-        @pl.when(hop == hops)
-        def _():
-            for part in range(2):
-                sib_copy(0, 0, part, 1 - core).wait_recv()
-
-        low = chip_at(spot - lax.rem(hop, hops))
-        high = chip_at(spot + hop)
+    def process(low, high):
         block = jnp.concatenate(
             [
                 rows[pl.ds(pl.multiple_of(chip * 2 * own_rows, 2 * own_rows), 2 * own_rows), :]
@@ -366,9 +402,50 @@
             def _():
                 base_recv[device] = piece
 
-        return carry
-
-    lax.fori_loop(1, hops + 1, step, 0)
+    def step(hop, carry):
+        def arrive(direction, part):
+            ring_arrival(direction, hop, part).wait_recv()
+            if part == direction:
+                pl.when(hop < hops)(lambda: ring_copy(direction, hop + 1, part).start())
+            else:
+                pl.when(hop < hops - 1)(lambda: ring_copy(direction, hop + 1, part).start())
+            sib_copy(direction, hop, part, core).start()
+
+        each_piece(hop, arrive)
+        each_piece(hop, lambda d, p: sib_copy(d, hop, p, 1 - core).wait_recv())
+
+        @pl.when(hop == hops)
+        def _():
+            for part in range(2):
+                sib_copy(0, 0, part, 1 - core).wait_recv()
+
+        process(chip_at(spot - lax.rem(hop, hops)), chip_at(spot + hop))
+        return carry
+
+    def receive(turn):
+        source = nearest(turn)
+        for part in range(2):
+            z_copy(source, True, part).wait_recv()
+            pass_on(source, part)
+
+    def line_step(turn, carry):
+        ahead = turn + 1 + middle * ((turn + 1) // 2)
+        pl.when(ahead <= last)(lambda: receive(ahead))
+        pl.when((middle == 1) & (turn == 0))(lambda: receive(2))
+        current = nearest(turn)
+        for part in range(2):
+            y_copy(current, 1 - side, part).wait_recv()
+            twin_copy(current * 2 + 1 - side, part, core).start()
+        for part in range(2):
+            twin_copy(current * 2 + side, part, 1 - core).wait_recv()
+            twin_copy(current * 2 + 1 - side, part, 1 - core).wait_recv()
+        process(current * 2, current * 2 + 1)
+        return carry
+
+    if block_2x4:
+        lax.fori_loop(0, last + 1, line_step, 0)
+    else:
+        lax.fori_loop(1, hops + 1, step, 0)
 
     def collect(offset, carry):
         device = lax.rem(me + offset, peers)
@@ -402,6 +479,18 @@
 
     lax.fori_loop(1, peers, finish, 0)
 
+    def line_drain(source, carry):
+        for part in range(2):
+            z_sends(source, part, lambda copy: copy.wait_send())
+            y_copy(source, side, part).wait_send()
+            for its_side in range(2):
+                twin_copy(source * 2 + its_side, part, core).wait_send()
+        return carry
+
+    if block_2x4:
+        lax.fori_loop(0, last + 1, line_drain, 0)
+        return
+
     for part in range(2):
         sib_copy(0, 0, part, core).wait_send()
 
@@ -416,7 +505,7 @@
     lax.fori_loop(1, hops + 1, drain, 0)
 
 
-def project(ids, lengths, queries, keys, values, weights, down, up, snake):
+def project(ids, lengths, queries, keys, values, weights, down, up, block_2x4):
     peers = lax.axis_size("ad")
     own_rows, width = queries.shape
     columns = weights.shape[1]
@@ -427,9 +516,9 @@
     hbm = pl.BlockSpec(memory_space=pl.ANY)
     dma = pltpu.SemaphoreType.DMA
     return pl.pallas_call(
-        functools.partial(project_kernel, peers, snake),
+        functools.partial(project_kernel, peers, block_2x4),
         out_shape=jax.ShapeDtypeStruct((own_rows, model_width), jnp.bfloat16),
-        in_specs=[vmem, vmem, smem, vmem, hbm, hbm, hbm, hbm, hbm],
+        in_specs=[vmem, smem, vmem, hbm, hbm, hbm, hbm, hbm],
         out_specs=vmem,
         scratch_shapes=[
             pltpu.VMEM((peers * own_rows, width), jnp.bfloat16),
@@ -445,8 +534,8 @@
             pltpu.VMEM((peers * PACK, model_width // FOLD), jnp.bfloat16),
             pltpu.VMEM((peers * PACK, model_width // FOLD), jnp.bfloat16),
             dma((7,)),
-            dma((hops * 4,)),
-            dma((hops * 4,)),
+            dma((hops * 4 + 8,)),
+            dma((hops * 4 + 8,)),
             dma(((hops + 1) * 4,)),
             dma(((hops + 1) * 4,)),
             dma((peers,)),
@@ -464,11 +553,11 @@
             bytes_accessed=2 * (weights.size + down.size + up.size),
             transcendentals=0,
         ),
-    )(ids.reshape(1, own_rows), ids.reshape(own_rows, 1), lengths, queries, keys, values, weights, down, up)
+    )(ids.reshape(1, own_rows), lengths, queries, keys, values, weights, down, up)
 
 
 def local(
-    snake,
+    block_2x4,
     queries,
     cached_key_vectors,
     stored_values,
@@ -487,7 +576,7 @@
         output_weight_rows,
         adapter_down_maps,
         adapter_up_maps,
-        snake,
+        block_2x4,
     )
 
 

time: 57.3 us -> 59.4 us (1.037)
  the two profiles are of different devices: /device:TPU:9 before, /device:TPU:7 now
where the time goes in v3:
time: 59.4 us; the launch traced here: 59.3 us
  Pallas kernels  57.4 us (97%)
  local copies, waits for them, and re-layouts  1.87 us (3%)
    pallas_call x1, Pallas kernels, project(): pl.pallas_call(functools.partial(project_kernel, peers, block_2x4), out_s...  57.4 us
    unnamed x1, local copies, waits for them, and re-layouts  1.87 us

profile of v3, /device:TPU:7, one launch (start us, length us, event | category | flops | bytes accessed | tf_op | source)
XLA Modules:
  0.0 59.3 jit_solution(12592712589345246760)
XLA Ops:
  0.0 57.4 %shard_map.82 = bf16[32,8192]{1,0:T(8,128)(2,1)} custom-call(s32[1,32]{1,0:T(1,128)} %bitcast.1, s32[32]{0:T(128)} %lengths_ref.1, bf16[32,4096]{1,0:T(8,128)(2,1)} %queries_ref.1, bf16[32,64,512]{2,1,0:T(8,128)(2,1)} %keys_hbm.1, bf16[32,64,512]{2,1,0:T(8,128)(2,1)} %values_hbm.1, bf16[4096,512]{1,0:T(8,128)(2,1)} %w_hbm.1, bf16[4096,256]{1,0:T(8,128)(2,1)} %down_hbm.1, ...), custom_call_target="tpu_custom_call" | custom-call | flops 3221225472 | bytes 10485760 | tf_op jit(solution)/shard_map/pallas_call | solution.py:518
  57.4 1.9 %copy.10 = bf16[32,8192]{1,0:T(8,128)(2,1)} copy(bf16[32,8192]{1,0:T(8,128)(2,1)} %shard_map.82) | data formatting | bytes 1048576

commit v4 on v2

--- a/solution.py
+++ b/solution.py
@@ -79,7 +79,6 @@
     peers,
     snake,
     ids_row_ref,
-    ids_col_ref,
     lengths_ref,
     queries_ref,
     keys_hbm,
@@ -169,12 +168,11 @@
     lax.fori_loop(1, peers, greet, 0)
 
     ids_row = ids_row_ref[...]
-    ids_col = ids_col_ref[...]
     owner_row = ids_row // share
-    owner_col = ids_col // share
-    same = owner_row == owner_col
     first = iota((own_rows, own_rows), 0)
     second = iota((own_rows, own_rows), 1)
+    owner_col = jnp.sum(jnp.where(first == second, owner_row, 0), axis=1, keepdims=True)
+    same = owner_row == owner_col
     rank_row = jnp.sum((same & (first < second)).astype(jnp.int32), axis=0, keepdims=True)
     rank_col = jnp.sum((same & (second < first)).astype(jnp.int32), axis=1, keepdims=True)
     slot_col = owner_col * CAP + rank_col
@@ -429,7 +427,7 @@
     return pl.pallas_call(
         functools.partial(project_kernel, peers, snake),
         out_shape=jax.ShapeDtypeStruct((own_rows, model_width), jnp.bfloat16),
-        in_specs=[vmem, vmem, smem, vmem, hbm, hbm, hbm, hbm, hbm],
+        in_specs=[vmem, smem, vmem, hbm, hbm, hbm, hbm, hbm],
         out_specs=vmem,
         scratch_shapes=[
             pltpu.VMEM((peers * own_rows, width), jnp.bfloat16),
@@ -464,7 +462,7 @@
             bytes_accessed=2 * (weights.size + down.size + up.size),
             transcendentals=0,
         ),
-    )(ids.reshape(1, own_rows), ids.reshape(own_rows, 1), lengths, queries, keys, values, weights, down, up)
+    )(ids.reshape(1, own_rows), lengths, queries, keys, values, weights, down, up)
 
 
 def local(

time: 57.3 us -> 55.9 us (0.976)
  local copies, waits for them, and re-layouts: 3.21 us -> 1.87 us
    reshape x1 -> x0, local copies, waits for them, and re-layouts: 1.34 us -> none  [project(): ids.reshape(own_rows, 1)]
where the time goes in v4:
time: 55.9 us; the launch traced here: 55.7 us
  Pallas kernels  53.8 us (96%)
  local copies, waits for them, and re-layouts  1.87 us (3%)
    pallas_call x1, Pallas kernels, project(): pl.pallas_call(functools.partial(project_kernel, peers, snake), out_shape...  53.8 us
    unnamed x1, local copies, waits for them, and re-layouts  1.87 us

profile of v4, /device:TPU:9, one launch (start us, length us, event | category | flops | bytes accessed | tf_op | source)
XLA Modules:
  0.0 55.7 jit_solution(8027538347592970387)
XLA Ops:
  0.0 53.8 %shard_map.82 = bf16[32,8192]{1,0:T(8,128)(2,1)} custom-call(s32[1,32]{1,0:T(1,128)} %bitcast.1, s32[32]{0:T(128)} %lengths_ref.1, bf16[32,4096]{1,0:T(8,128)(2,1)} %queries_ref.1, bf16[32,64,512]{2,1,0:T(8,128)(2,1)} %keys_hbm.1, bf16[32,64,512]{2,1,0:T(8,128)(2,1)} %values_hbm.1, bf16[4096,512]{1,0:T(8,128)(2,1)} %w_hbm.1, bf16[4096,256]{1,0:T(8,128)(2,1)} %down_hbm.1, ...), custom_call_target="tpu_custom_call" | custom-call | flops 3221225472 | bytes 10485760 | tf_op jit(solution)/shard_map/pallas_call | solution.py:427
  53.8 1.9 %copy.10 = bf16[32,8192]{1,0:T(8,128)(2,1)} copy(bf16[32,8192]{1,0:T(8,128)(2,1)} %shard_map.82) | data formatting | bytes 1048576
